TPU v7x, 512 devices: a whole 4x8x8 slice. The times are simulated.
512 devices in a mesh: dp: 8 (over y), expert: 64 (over x, z, core).
Axes of the slice: x: 4, y: 8, z: 8, core: 2. Of those that a mesh axis runs over, the one named last changes fastest.
Arguments:
- tokens: bfloat16 [32768, 1024], P(('dp', 'expert')), may hold values from -6 to 6
- expert_ids: int32 [32768, 8], P(('dp', 'expert')), may hold values from 0 to 63, all different within a row; in each aligned block of 64 rows (0 to 63, 64 to 127, ...) at most 10 rows name the same one
- gate_values: float32 [32768, 8], P(('dp', 'expert')), may hold values from 0.05 to 0.5
- cotangent: bfloat16 [32768, 1024], P(('dp', 'expert')), may hold values from -6 to 6
- w_gate: bfloat16 [64, 1024, 512], P('expert'), may hold values from -0.1875 to 0.1875
- w_up: bfloat16 [64, 1024, 512], P('expert'), may hold values from -0.1875 to 0.1875
- w_down: bfloat16 [64, 512, 1024], P('expert'), may hold values from -0.25 to 0.25
Outputs:
- layer_output: bfloat16 [32768, 1024], P(('dp', 'expert'))
- d_tokens: bfloat16 [32768, 1024], P(('dp', 'expert'))
- d_gate_w: float32 [64, 1024, 512], P('expert', 'dp')
- d_up_w: float32 [64, 1024, 512], P('expert', 'dp')
- d_down_w: float32 [64, 512, 1024], P('expert', None, 'dp')
Inputs may be any that keep to these rules, and one draw needn't show every extreme that they name: `expert_ids`: the 8 ids of a row are distinct. In each aligned block of 64 rows (the tokens of one device) no expert is named by more than 10 rows, a bound that some block reaches.
All inputs are finite; a program needn't handle non-finite values.
Results may differ from a plain program's by a relative error of at most 0.015.
Values may be sent and summed in bfloat16 or wider, within the bound.
A program may use at most 64 MiB of HBM per device.

v0:
```python
import jax
import jax.numpy as jnp
from jax import lax
from jax.sharding import PartitionSpec as P


def contract(left_side, right_side):
    return lax.dot_general(
        left_side, right_side, (((0,), (0,)), ((), ())), preferred_element_type=jnp.float32
    )


def backward_rows(grad_rows, gate_pre, up_pre, gate_mat, up_mat, down_mat):
    sigmoid_gate = jax.nn.sigmoid(gate_pre)
    activation = (gate_pre * sigmoid_gate * up_pre).astype(jnp.bfloat16)
    d_activation = lax.dot_general(
        grad_rows, down_mat, (((1,), (1,)), ((), ())), preferred_element_type=jnp.float32
    )
    d_up_pre = (d_activation * gate_pre * sigmoid_gate).astype(jnp.bfloat16)
    d_gate_pre = (
        d_activation * up_pre * sigmoid_gate * (1.0 + gate_pre * (1.0 - sigmoid_gate))
    ).astype(jnp.bfloat16)
    input_grads = (
        lax.dot_general(
            d_gate_pre, gate_mat, (((1,), (1,)), ((), ())), preferred_element_type=jnp.float32
        )
        + lax.dot_general(
            d_up_pre, up_mat, (((1,), (1,)), ((), ())), preferred_element_type=jnp.float32
        )
    ).astype(jnp.bfloat16)
    return (activation, d_gate_pre, d_up_pre, input_grads)


def on_device(tokens, expert_ids, gate_values, cotangent, w_gate, w_up, w_down):
    experts = lax.axis_size("expert")
    tok_count, top_count = expert_ids.shape
    features = tokens.shape[1]
    capacity = min(tok_count, max(2, 5 * tok_count * top_count // (4 * experts)))
    pair_count = tok_count * top_count
    gate_mat = w_gate[0]
    up_mat = w_up[0]
    down_mat = w_down[0]
    hidden = gate_mat.shape[1]
    flat_ids = expert_ids.reshape(-1)
    onehot = (flat_ids[:, None] == jnp.arange(experts, dtype=jnp.int32)[None, :]).astype(jnp.int32)
    before = jnp.cumsum(onehot, axis=0) - onehot
    slot_index = jnp.sum(before * onehot, axis=1)
    target = flat_ids * capacity + slot_index
    source = jnp.arange(pair_count, dtype=jnp.int32) // top_count
    outgoing = (
        jnp.zeros((experts * capacity, features), jnp.bfloat16).at[target].set(tokens[source])
    )
    outgoing = outgoing.reshape(experts, capacity, features)
    scaled = (gate_values[:, :, None] * cotangent[:, None, :].astype(jnp.float32)).astype(
        jnp.bfloat16
    )
    grad_out = (
        jnp.zeros((experts * capacity, features), jnp.bfloat16)
        .at[target]
        .set(scaled.reshape(pair_count, features))
    )
    grad_out = grad_out.reshape(experts, capacity, features)
    received = lax.all_to_all(outgoing, "expert", split_axis=0, concat_axis=0, tiled=True)
    forward_input_rows = received.reshape(-1, features)
    gate_pre = jnp.dot(forward_input_rows, gate_mat, preferred_element_type=jnp.float32)
    up_pre = jnp.dot(forward_input_rows, up_mat, preferred_element_type=jnp.float32)
    forward_activation = (gate_pre * jax.nn.sigmoid(gate_pre) * up_pre).astype(jnp.bfloat16)
    produced = jnp.dot(forward_activation, down_mat, preferred_element_type=jnp.float32).astype(
        jnp.bfloat16
    )
    returned = lax.all_to_all(
        produced.reshape(received.shape), "expert", split_axis=0, concat_axis=0, tiled=True
    )
    hidden_shape = (received.shape[0], received.shape[1], hidden)
    returned, received, gate_keep, up_keep = (
        returned,
        received,
        gate_pre.reshape(hidden_shape),
        up_pre.reshape(hidden_shape),
    )
    grad_in = lax.all_to_all(grad_out, "expert", split_axis=0, concat_axis=0, tiled=True)
    input_rows = received.reshape(-1, features)
    grad_rows = grad_in.reshape(-1, features)
    activation, d_gate_pre, d_up_pre, input_grads = backward_rows(
        grad_rows,
        gate_keep.reshape(-1, hidden),
        up_keep.reshape(-1, hidden),
        gate_mat,
        up_mat,
        down_mat,
    )
    returned_grads = lax.all_to_all(
        input_grads.reshape(experts, capacity, features),
        "expert",
        split_axis=0,
        concat_axis=0,
        tiled=True,
    )
    picked = returned.reshape(experts * capacity, features)[target].reshape(
        tok_count, top_count, features
    )
    layer_output = jnp.einsum("tk,tkd->td", gate_values, picked.astype(jnp.float32)).astype(
        jnp.bfloat16
    )
    gathered_grads = returned_grads.reshape(experts * capacity, features)[target].reshape(
        tok_count, top_count, features
    )
    d_tokens = jnp.sum(gathered_grads.astype(jnp.float32), axis=1).astype(jnp.bfloat16)
    both_pre = jnp.concatenate([d_gate_pre, d_up_pre], axis=1)
    gate_up_sum = lax.psum_scatter(
        contract(input_rows, both_pre).astype(jnp.bfloat16), "dp", scatter_dimension=0, tiled=True
    ).astype(jnp.float32)
    down_sum = lax.psum_scatter(
        contract(grad_rows, activation).astype(jnp.bfloat16), "dp", scatter_dimension=0, tiled=True
    ).astype(jnp.float32)
    d_gate_w = gate_up_sum[:, :hidden][None]
    d_up_w = gate_up_sum[:, hidden:][None]
    d_down_w = down_sum.T[None]
    return (layer_output, d_tokens, d_gate_w, d_up_w, d_down_w)


def solution(mesh):
    placed = (
        P(("dp", "expert"), None),
        P(("dp", "expert"), None),
        P(("dp", "expert"), None),
        P(("dp", "expert"), None),
        P("expert", None, None),
        P("expert", None, None),
        P("expert", None, None),
    )
    return jax.shard_map(
        on_device,
        mesh=mesh,
        in_specs=placed,
        out_specs=(
            P(("dp", "expert"), None),
            P(("dp", "expert"), None),
            P("expert", "dp", None),
            P("expert", "dp", None),
            P("expert", None, "dp"),
        ),
        check_vma=False,
    )
```

profile of v0, /device:TPU:1, one launch (start us, length us, event | category | flops | bytes accessed | tf_op | source)
XLA Modules:
  0.0 284.8 jit_solution(8380291963268707148)
XLA Ops:
  10.8 7.6 %scatter_custom_fusion = bf16[640,1024]{1,0:T(8,128)(2,1)S(1)} fusion(s32[512]{0:T(512)S(1)} %bitcast.76, bf16[64,1024]{1,0:T(8,128)(2,1)} %param.7, s32[1024]{0:T(1024)S(1)} %pad_clamp_fusion.1, bf16[]{:T(256)} %constant.26.clone.1), kind=kCustom, calls=%fused_computation.32 | custom fusion | bytes 1311232 | tf_op jit(solution)/shard_map/scatter | solution.py:51
  19.9 15.0 %all-to-all-start = ((bf16[64,10,1024]{2,1,0:T(8,128)(2,1)}), bf16[64,10,1024]{2,1,0:T(8,128)(2,1)S(1)}, u32[]{:S(2)}, u32[]{:S(2)}) async-start(bf16[64,10,1024]{2,1,0:T(8,128)(2,1)} %reshape.138), calls=%async_computation | async-start | bytes 4194304 | tf_op jit(solution)/shard_map/all_to_all | solution.py:63
  35.1 3.8 %scatter_custom_fusion.1 = bf16[640,1024]{1,0:T(8,128)(2,1)} fusion(s32[512]{0:T(512)S(1)} %bitcast.77, f32[64,1024]{1,0:T(8,128)S(1)} %convert_element_type.52, f32[512]{0:T(512)S(1)} %mul.69, bf16[]{:T(256)} %constant.26.clone.1), kind=kCustom, calls=%fused_computation.18 | custom fusion | flops 1048576 | bytes 1574914 | tf_op jit(solution)/shard_map/scatter | solution.py:60
  38.8 3.6 %reshape.143 = bf16[64,10,1024]{2,1,0:T(8,128)(2,1)} reshape(bf16[640,1024]{1,0:T(8,128)(2,1)} %scatter_custom_fusion.1) | data formatting | bytes 2621440 | tf_op jit(solution)/shard_map/reshape | solution.py:62
  42.4 43.7 %all-to-all-done = bf16[64,10,1024]{2,1,0:T(8,128)(2,1)S(1)} async-done(((bf16[64,10,1024]{2,1,0:T(8,128)(2,1)}), bf16[64,10,1024]{2,1,0:T(8,128)(2,1)S(1)}, u32[]{:S(2)}, u32[]{:S(2)}) %all-to-all-start) | async-done | bytes 1310752 | tf_op jit(solution)/shard_map/all_to_all | solution.py:63
  86.1 6.0 %all-to-all-start.2 = ((bf16[64,10,1024]{2,1,0:T(8,128)(2,1)}), bf16[64,10,1024]{2,1,0:T(8,128)(2,1)}, u32[]{:S(2)}, u32[]{:S(2)}) async-start(bf16[64,10,1024]{2,1,0:T(8,128)(2,1)} %reshape.143), calls=%async_computation.2 | async-start | bytes 4194304 | tf_op jit(solution)/shard_map/all_to_all | solution.py:81
  93.7 3.9 %fusion.12 = f32[640,512]{0,1:T(8,128)} fusion(bf16[640,1024]{1,0:T(8,128)(2,1)} %reshape.139, bf16[1,1024,512]{2,1,0:T(8,128)(2,1)} %param.12), kind=kOutput, calls=%fused_computation.26 | convolution fusion | flops 671088640 | bytes 3670016 | tf_op jit(solution)/shard_map/dot_general | solution.py:66
  97.6 2.1 fusion.16
  99.7 43.6 %all-to-all-done.2 = bf16[64,10,1024]{2,1,0:T(8,128)(2,1)} async-done(((bf16[64,10,1024]{2,1,0:T(8,128)(2,1)}), bf16[64,10,1024]{2,1,0:T(8,128)(2,1)}, u32[]{:S(2)}, u32[]{:S(2)}) %all-to-all-start.2) | async-done | bytes 1310752 | tf_op jit(solution)/shard_map/all_to_all | solution.py:81
  143.3 2.6 reshape.144
  145.9 4.2 %multiply_convert_fusion = (bf16[640,512]{0,1:T(8,128)(2,1)}, bf16[640,512]{0,1:T(8,128)(2,1)}, bf16[640,512]{0,1:T(8,128)(2,1)S(1)}) fusion(f32[640,512]{0,1:T(8,128)} %fusion.16, f32[640,512]{0,1:T(8,128)} %fusion.12, bf16[640,1024]{1,0:T(8,128)(2,1)S(1)} %reshape.144, bf16[1,512,1024]{2,1,0:T(8,128)(2,1)S(1)} %copy-done), kind=kOutput, calls=%fused_computation.14 | convolution fusion | flops 676331520 | bytes 6946816 | tf_op jit(solution)/shard_map/dot_general | solution.py:16
  150.1 2.0 convolution_convert_fusion.2
  154.5 5.8 %all-to-all-start.1 = ((bf16[64,10,1024]{2,1,0:T(8,128)(2,1)}), bf16[64,10,1024]{2,1,0:T(8,128)(2,1)S(1)}, u32[]{:S(2)}, u32[]{:S(2)}) async-start(bf16[64,10,1024]{2,1,0:T(8,128)(2,1)} %reshape.140), calls=%async_computation.1 | async-start | bytes 4194304 | tf_op jit(solution)/shard_map/all_to_all | solution.py:71
  160.4 4.9 %convolution_convert_fusion = bf16[1024,1024]{1,0:T(8,128)(2,1)} fusion(bf16[640,1024]{1,0:T(8,128)(2,1)} %reshape.139, bf16[640,512]{0,1:T(8,128)(2,1)} %get-tuple-element.15, bf16[640,512]{0,1:T(8,128)(2,1)} %get-tuple-element.16), kind=kOutput, calls=%fused_computation.8 | convolution fusion | flops 1345847296 | bytes 4718592 | tf_op jit(solution)/shard_map/dot_general | solution.py:8
  165.3 2.4 fusion.14
  167.8 2.0 add_convert_fusion
  169.8 3.6 %reshape.145 = bf16[64,10,1024]{2,1,0:T(8,128)(2,1)} reshape(bf16[640,1024]{1,0:T(8,128)(2,1)} %add_convert_fusion) | data formatting | bytes 2621440 | tf_op jit(solution)/shard_map/reshape | solution.py:93
  173.4 38.2 %all-to-all-done.1 = bf16[64,10,1024]{2,1,0:T(8,128)(2,1)S(1)} async-done(((bf16[64,10,1024]{2,1,0:T(8,128)(2,1)}), bf16[64,10,1024]{2,1,0:T(8,128)(2,1)S(1)}, u32[]{:S(2)}, u32[]{:S(2)}) %all-to-all-start.1) | async-done | bytes 1310752 | tf_op jit(solution)/shard_map/all_to_all | solution.py:71
  213.0 6.0 %all-to-all-start.3 = ((bf16[64,10,1024]{2,1,0:T(8,128)(2,1)}), bf16[64,10,1024]{2,1,0:T(8,128)(2,1)}, u32[]{:S(2)}, u32[]{:S(2)}) async-start(bf16[64,10,1024]{2,1,0:T(8,128)(2,1)} %reshape.145), calls=%async_computation.3 | async-start | bytes 4194304 | tf_op jit(solution)/shard_map/all_to_all | solution.py:92
  220.9 2.6 reshape.141
  223.5 2.1 gather_fusion
  226.7 43.4 %all-to-all-done.3 = bf16[64,10,1024]{2,1,0:T(8,128)(2,1)} async-done(((bf16[64,10,1024]{2,1,0:T(8,128)(2,1)}), bf16[64,10,1024]{2,1,0:T(8,128)(2,1)}, u32[]{:S(2)}, u32[]{:S(2)}) %all-to-all-start.3) | async-done | bytes 1310752 | tf_op jit(solution)/shard_map/all_to_all | solution.py:92
  270.2 2.6 reshape.146
  272.7 2.1 gather_fusion.1
  (53 shorter events, 16.9 us)
Async XLA Ops:
  7.2 138.7 %copy-start = (bf16[1,512,1024]{2,1,0:T(8,128)(2,1)S(1)}, bf16[1,512,1024]{2,1,0:T(8,128)(2,1)}, u32[]{:S(2)}) copy-start(bf16[1,512,1024]{2,1,0:T(8,128)(2,1)} %param.13) | copy-start | bytes 3145732
  19.9 15.0 %copy-start.7 = (f32[64,8]{0,1:T(8,128)S(1)}, f32[64,8]{0,1:T(8,128)}, u32[]{:S(2)}) copy-start(f32[64,8]{0,1:T(8,128)} %param.9) | copy-start | bytes 6148
  19.9 15.2 %copy-start.6 = (bf16[64,1024]{1,0:T(8,128)(2,1)S(1)}, bf16[64,1024]{1,0:T(8,128)(2,1)}, u32[]{:S(2)}) copy-start(bf16[64,1024]{1,0:T(8,128)(2,1)} %param.10) | copy-start | bytes 393220
  19.9 66.2 %all-to-all-start = ((bf16[64,10,1024]{2,1,0:T(8,128)(2,1)}), bf16[64,10,1024]{2,1,0:T(8,128)(2,1)S(1)}, u32[]{:S(2)}, u32[]{:S(2)}) async-start(bf16[64,10,1024]{2,1,0:T(8,128)(2,1)} %reshape.138), calls=%async_computation | async-start | bytes 4194304 | tf_op jit(solution)/shard_map/all_to_all | solution.py:63
  86.1 57.2 %all-to-all-start.2 = ((bf16[64,10,1024]{2,1,0:T(8,128)(2,1)}), bf16[64,10,1024]{2,1,0:T(8,128)(2,1)}, u32[]{:S(2)}, u32[]{:S(2)}) async-start(bf16[64,10,1024]{2,1,0:T(8,128)(2,1)} %reshape.143), calls=%async_computation.2 | async-start | bytes 4194304 | tf_op jit(solution)/shard_map/all_to_all | solution.py:81
  92.1 127.0 %reduce-scatter.5.cloned.1.call-start = ((), (), s32[]{:S(2)}) async-start(), calls=%async_computation.7 | async-start | bytes 1179648 | tf_op jit(solution)/shard_map/reduce_scatter | solution.py:113
  93.7 3.9 %copy-start.2 = (bf16[640,1024]{1,0:T(8,128)(2,1)S(1)}, bf16[640,1024]{1,0:T(8,128)(2,1)}, u32[]{:S(2)}) copy-start(bf16[640,1024]{1,0:T(8,128)(2,1)} %reshape.139) | copy-start | bytes 3932164
  93.7 3.9 %copy-start.3 = (bf16[1,1024,512]{2,1,0:T(8,128)(2,1)S(1)}, bf16[1,1024,512]{2,1,0:T(8,128)(2,1)}, u32[]{:S(2)}) copy-start(bf16[1,1024,512]{2,1,0:T(8,128)(2,1)} %param.11) | copy-start | bytes 3145732
  154.5 57.1 %all-to-all-start.1 = ((bf16[64,10,1024]{2,1,0:T(8,128)(2,1)}), bf16[64,10,1024]{2,1,0:T(8,128)(2,1)S(1)}, u32[]{:S(2)}, u32[]{:S(2)}) async-start(bf16[64,10,1024]{2,1,0:T(8,128)(2,1)} %reshape.140), calls=%async_computation.1 | async-start | bytes 4194304 | tf_op jit(solution)/shard_map/all_to_all | solution.py:71
  160.3 115.8 %reduce-scatter.3.cloned.1.call-start = ((), (), s32[]{:S(2)}) async-start(), calls=%async_computation.6 | async-start | bytes 2359296 | tf_op jit(solution)/shard_map/reduce_scatter | solution.py:110
  165.3 2.5 copy-start.4
  165.3 2.5 copy-start.5
  211.6 1.4 copy-start.1
  213.0 57.2 %all-to-all-start.3 = ((bf16[64,10,1024]{2,1,0:T(8,128)(2,1)}), bf16[64,10,1024]{2,1,0:T(8,128)(2,1)}, u32[]{:S(2)}, u32[]{:S(2)}) async-start(bf16[64,10,1024]{2,1,0:T(8,128)(2,1)} %reshape.145), calls=%async_computation.3 | async-start | bytes 4194304 | tf_op jit(solution)/shard_map/all_to_all | solution.py:92
Sparse Core Ops, SparseCore 0:
  152.2 33.4 reduce-scatter.4
  188.5 43.6 reduce-scatter.2
where the time goes:
time: 286 us; the launch traced here: 285 us
  waiting for transfers between devices  169 us (59%)
  local copies, waits for them, and re-layouts  36.5 us (13%)
  starting transfers between devices  33.1 us (12%)
  matrix products  22.8 us (8%)
  between operations  14.3 us (5%)
  other arithmetic  9.23 us (3%)
    all_to_all x1, waiting for transfers between devices, on_device(): lax.all_to_all(outgoing, 'expert', split_axis=0, concat_axis=0, tiled=True)  43.7 us
    all_to_all x1, waiting for transfers between devices, on_device(): lax.all_to_all(grad_out, 'expert', split_axis=0, concat_axis=0, tiled=True)  43.6 us
    all_to_all x1, waiting for transfers between devices, on_device(): lax.all_to_all(input_grads.reshape(experts, capacity, features), 'expert'...  43.4 us
    all_to_all x1, waiting for transfers between devices, on_device(): lax.all_to_all(produced.reshape(received.shape), 'expert', split_axis=0,...  38.2 us
    all_to_all x1, starting transfers between devices, on_device(): lax.all_to_all(outgoing, 'expert', split_axis=0, concat_axis=0, tiled=True)  15 us
    scatter x1, local copies, waits for them, and re-layouts, on_device(): jnp.zeros((experts * capacity, features), jnp.bfloat16).at[target]  7.59 us
    dot_general x2, matrix products, contract(): lax.dot_general(left_side, right_side, (((0,), (0,)), ((), ())), preferre...  6.87 us
    all_to_all x1, starting transfers between devices, on_device(): lax.all_to_all(input_grads.reshape(experts, capacity, features), 'expert'...  6.02 us
  transfers between devices with their start and end apart: 6, of which 4 were waited for; matrix products, arithmetic and copies ran while one was open for 15% of the time, Pallas kernels for 0%

commit v1 on v0

v1 whole, which is shorter than its diff:
```python
import jax
import jax.numpy as jnp
from jax import lax
from jax.experimental import pallas as pl
from jax.experimental.pallas import tpu as pltpu
from jax.sharding import PartitionSpec as P

MESH = pl.DeviceIdType.MESH
BF = jnp.bfloat16
F32 = jnp.float32
NX, NZ, NC = 4, 8, 2
NY = 8
TOK = 64
D = 1024
HALF = D // 2
FF = 512
CAP = 10
SLOTS = NZ * CAP
PEERS = NX * NC
ROWS = PEERS * SLOTS
GATHERED = NZ * TOK
EXPERTS = NX * NZ * NC
TILE = 160
STEPS = ((4, 3), (3, 4))
WROWS = 192


def nn(a, b):
    return jnp.dot(a, b, preferred_element_type=F32)


def nt(a, b):
    return lax.dot_general(a, b, (((1,), (1,)), ((), ())), preferred_element_type=F32)


def tn(a, b):
    return lax.dot_general(a, b, (((0,), (0,)), ((), ())), preferred_element_type=F32)


def kernel(
    ids_ref, gv_ref, tok_ref, cot_ref, wg_ref, wu_ref, wd_ref,
    out_ref, dtok_ref, dg_ref, du_ref, dd_ref,
    meta, gath, pick, pick_t, pickg_t, gslot, send_x, recv_x, keep_s, keep_d, act, dpre, part, zbuf, wpart, ybuf,
    m_ss, m_rs, g_ss, g_rs, x_ss, x_rs, z_ss, z_rs, y_ss, y_rs,
):
    y = lax.axis_index("dp")
    e = lax.axis_index("expert")
    c = e % 2
    z = (e // 2) % NZ
    x = e // (2 * NZ)
    up = (y, (x * NZ + (z + 1) % NZ) * 2 + c)
    down = (y, (x * NZ + (z + NZ - 1) % NZ) * 2 + c)
    y_up = ((y + 1) % NY, e)
    y_down = ((y + NY - 1) % NY, e)

    def peer(j, sign):
        dx, dc = j // 2, j % 2
        return (y, (((x + sign * dx + NX) % NX) * NZ + z) * 2 + (c + dc) % 2)

    barrier = pltpu.get_barrier_semaphore()
    friends = [up, down, y_up, y_down] + [peer(j, 1) for j in range(1, PEERS)]
    for friend in friends:
        pl.semaphore_signal(barrier, inc=1, device_id=friend, device_id_type=MESH)

    lane = lax.broadcasted_iota(jnp.int32, (TOK, 2 * EXPERTS), 1)
    gate = jnp.zeros((TOK, 2 * EXPERTS), F32)
    for k in range(8):
        gate = jnp.where(lane % EXPERTS == ids_ref[:, k : k + 1], gv_ref[:, k : k + 1], gate)
    high = gate.astype(BF).astype(F32)
    meta[0] = jnp.where(lane < EXPERTS, high, gate - high).astype(BF)
    for h in range(2):
        gath[0, h, 0] = tok_ref[:, h * HALF : (h + 1) * HALF]
        gath[1, h, 0] = cot_ref[:, h * HALF : (h + 1) * HALF]

    pl.semaphore_wait(barrier, len(friends))

    started = []

    def send(src, dst, ss, rs, to):
        copy = pltpu.make_async_remote_copy(
            src_ref=src, dst_ref=dst, send_sem=ss, recv_sem=rs, device_id=to, device_id_type=MESH
        )
        copy.start()
        started.append(copy)
        return copy

    def gather_step(buf, ss, rs, steps, s, prev):
        now = []
        for way, (to, count) in enumerate(zip((up, down), steps)):
            if s > count:
                now.append(None)
                continue
            if s > 1:
                prev[way].wait_recv()
            src = (NZ - s + 1) % NZ if way == 0 else s - 1
            dst = NZ - s if way == 0 else s
            now.append(send(buf.at[src], buf.at[dst], ss.at[dst], rs.at[dst], to))
        return [n if n is not None else p for n, p in zip(now, prev or (None, None))]

    m_last, t_last, c_last = None, [None, None], [None, None]
    for s in range(1, 5):
        m_last = gather_step(meta, m_ss, m_rs, STEPS[0], s, m_last)
        for h in range(2):
            t_last[h] = gather_step(gath.at[0, h], g_ss.at[0, h], g_rs.at[0, h], STEPS[h], s, t_last[h])
    for h in range(2):
        c_last[h] = gather_step(gath.at[1, h], g_ss.at[1, h], g_rs.at[1, h], STEPS[h], 1, None)

    for way in range(2):
        m_last[way].wait_recv()
    row = lax.broadcasted_iota(jnp.int32, (16, 2 * EXPERTS), 0)
    col = lax.broadcasted_iota(jnp.int32, (16, 2 * EXPERTS), 1)
    wanted = (((x + (row % PEERS) // 2) % NX) * NZ + z) * 2 + (c + row) % 2
    chosen = jnp.where(col % EXPERTS == wanted, 1.0, 0.0).astype(BF)
    gate_row = nt(chosen, meta[...].reshape(GATHERED, 2 * EXPERTS))
    match = jnp.where(gate_row > 0.0, 1.0, 0.0)
    first = lax.broadcasted_iota(jnp.int32, (GATHERED, GATHERED), 0)
    second = lax.broadcasted_iota(jnp.int32, (GATHERED, GATHERED), 1)
    rank = nn(match.astype(BF), jnp.where(first < second, 1.0, 0.0).astype(BF))
    place = jnp.where(gate_row > 0.0, rank, -1.0)
    slot = lax.broadcasted_iota(jnp.int32, (SLOTS, GATHERED), 0).astype(F32)
    for j in range(PEERS):
        hit = slot == place[j : j + 1, :]
        pick[j * SLOTS : (j + 1) * SLOTS, :] = jnp.where(hit, 1.0, 0.0).astype(BF)
        weight = jnp.sum(jnp.where(hit, gate_row[j : j + 1, :], 0.0), axis=1, keepdims=True)
        gslot[j * SLOTS : (j + 1) * SLOTS, :] = jnp.broadcast_to(weight, (SLOTS, 128))

    for h in range(2):
        for way in range(2):
            t_last[h][way].wait_recv()

    def tiles(body):
        def step(i, carry):
            body(pl.ds(pl.multiple_of(i * TILE, 16), TILE))
            return carry

        lax.fori_loop(0, ROWS // TILE, step, 0)

    def exchange(n, src, dst, sign):
        own = pl.ds(0, SLOTS)
        dst[own, :] = src[own, :]
        copies = []
        for j in (4, 5, 2, 3, 6, 7, 1):
            block = pl.ds(j * SLOTS, SLOTS)
            copies.append(send(src.at[block], dst.at[block], x_ss.at[n, j], x_rs.at[n, j], peer(j, sign)))
        return copies

    def pick_tokens(rows):
        for h in range(2):
            source = gath[0, h].reshape(GATHERED, HALF)
            send_x[0, rows, h * HALF : (h + 1) * HALF] = nn(pick[rows, :], source).astype(BF)

    tiles(pick_tokens)
    tok_moves = exchange(0, send_x.at[0], recv_x.at[0], 1)

    for s in range(2, 5):
        for h in range(2):
            c_last[h] = gather_step(gath.at[1, h], g_ss.at[1, h], g_rs.at[1, h], STEPS[h], s, c_last[h])
    for h in range(2):
        for way in range(2):
            c_last[h][way].wait_recv()

    def pick_grads(rows):
        for h in range(2):
            source = gath[1, h].reshape(GATHERED, HALF)
            scaled = nn(pick[rows, :], source) * gslot[rows, 0:1]
            send_x[1, rows, h * HALF : (h + 1) * HALF] = scaled.astype(BF)

    tiles(pick_grads)
    cot_moves = exchange(1, send_x.at[1], recv_x.at[1], 1)

    for q in range(4):
        cols = slice(q * 128, (q + 1) * 128)
        plain = pick[:, cols].astype(F32)
        pick_t[cols, :] = plain.T.astype(BF)
        pickg_t[cols, :] = (plain * gslot[...]).T.astype(BF)

    for move in tok_moves:
        move.wait_recv()

    def forward(rows):
        inp = recv_x[0, rows, :]
        g = nn(inp, wg_ref[...])
        u = nn(inp, wu_ref[...])
        s = jax.nn.sigmoid(g)
        silu = g * s
        keep_s[rows, :] = silu
        keep_d[rows, :] = u * s * (1.0 + g * (1.0 - s))
        a = (silu * u).astype(BF)
        act[rows, :] = a
        send_x[2, rows, :] = nn(a, wd_ref[...]).astype(BF)

    tiles(forward)

    for move in cot_moves:
        move.wait_recv()
    out_moves = exchange(2, send_x.at[2], recv_x.at[2], -1)

    def backward(rows):
        da = nt(recv_x[1, rows, :], wd_ref[...])
        d_up = (da * keep_s[rows, :]).astype(BF)
        d_gate = (da * keep_d[rows, :]).astype(BF)
        dpre[rows, 0:FF] = d_gate
        dpre[rows, FF : 2 * FF] = d_up
        send_x[3, rows, :] = (nt(d_gate, wg_ref[...]) + nt(d_up, wu_ref[...])).astype(BF)

    tiles(backward)
    grad_moves = exchange(3, send_x.at[3], recv_x.at[3], -1)

    def weight_part(k):
        cols = pl.ds(pl.multiple_of(((y + k) % NY) * 128, 128), 128)
        both = tn(recv_x[0, :, cols], dpre[...])
        wpart[k, 0:128, :] = both[:, 0:FF]
        wpart[k, 128:256, :] = both[:, FF : 2 * FF]
        wpart[k, 256:384, :] = tn(recv_x[1, :, cols], act[...])

    def reduce_step(buf, ss, rs, ways, h, s, prev, own):
        now = []
        for way in range(2):
            count = STEPS[h][way]
            if s > count:
                now.append(prev[way])
                continue
            ahead = count + 1 - s
            term = own(ahead if way == 0 else 8 - ahead, h)
            if s > 1:
                prev[way].wait_recv()
                term = term + buf[h, way, s - 1].astype(F32)
            buf[h, way, s - 1] = term.astype(BF)
            now.append(
                send(buf.at[h, way, s - 1], buf.at[h, way, s], ss.at[h, way, s], rs.at[h, way, s], ways[way])
            )
        return now

    def reduce_end(buf, h, prev, own):
        for way in range(2):
            prev[way].wait_recv()
        first, second = STEPS[h]
        return own(0, h) + buf[h, 0, first].astype(F32) + buf[h, 1, second].astype(F32)

    def own_w(k, h):
        return wpart[k, h * WROWS : (h + 1) * WROWS, :]

    def own_part(a):
        return lambda k, h: part[a, k * TOK : (k + 1) * TOK, h * HALF : (h + 1) * HALF]

    y_last, z_last = [None, None], [[None, None], [None, None]]

    def y_step(s):
        for h in range(2):
            y_last[h] = reduce_step(ybuf, y_ss, y_rs, (y_up, y_down), h, s, y_last[h], own_w)

    def z_step(a, s):
        for h in range(2):
            z_last[a][h] = reduce_step(
                zbuf.at[a], z_ss.at[a], z_rs.at[a], (up, down), h, s, z_last[a][h], own_part(a)
            )

    def combine(a, weights, moves):
        for move in moves:
            move.wait_recv()

        def step(i, carry):
            rows = pl.ds(pl.multiple_of(i * 128, 128), 128)
            part[a, rows, :] = nn(weights[rows, :], recv_x[2 + a])
            return carry

        lax.fori_loop(0, GATHERED // 128, step, 0)

    def z_end(a, result):
        for h in range(2):
            result[:, h * HALF : (h + 1) * HALF] = reduce_end(zbuf.at[a], h, z_last[a][h], own_part(a)).astype(BF)

    weight_part(4)
    weight_part(3)
    weight_part(5)
    y_step(1)
    combine(0, pickg_t, out_moves)
    z_step(0, 1)
    for k in (2, 6, 1, 7, 0):
        weight_part(k)
    z_step(0, 2)
    y_step(2)
    z_step(0, 3)
    z_step(0, 4)
    combine(1, pick_t, grad_moves)
    z_step(1, 1)
    y_step(3)
    z_step(1, 2)
    z_end(0, out_ref)
    z_step(1, 3)
    y_step(4)
    z_step(1, 4)
    z_end(1, dtok_ref)
    low = reduce_end(ybuf, 0, y_last[0], own_w)
    dg_ref[...] = low[0:128]
    du_ref[0:64] = low[128:192]
    rest = reduce_end(ybuf, 1, y_last[1], own_w)
    du_ref[64:128] = rest[0:64]
    dd_ref[...] = rest[64:192].T

    for copy in started:
        copy.wait_send()


def on_device(tokens, expert_ids, gate_values, cotangent, w_gate, w_up, w_down):
    vmem = pl.BlockSpec(memory_space=pltpu.VMEM)
    dma = pltpu.SemaphoreType.DMA
    out, dtok, dg, du, dd = pl.pallas_call(
        kernel,
        out_shape=(
            jax.ShapeDtypeStruct((TOK, D), BF),
            jax.ShapeDtypeStruct((TOK, D), BF),
            jax.ShapeDtypeStruct((128, FF), F32),
            jax.ShapeDtypeStruct((128, FF), F32),
            jax.ShapeDtypeStruct((FF, 128), F32),
        ),
        in_specs=[vmem] * 7,
        out_specs=(vmem,) * 5,
        scratch_shapes=[
            pltpu.VMEM((NZ, TOK, 2 * EXPERTS), BF),
            pltpu.VMEM((2, 2, NZ, TOK, HALF), BF),
            pltpu.VMEM((ROWS, GATHERED), BF),
            pltpu.VMEM((GATHERED, ROWS), BF),
            pltpu.VMEM((GATHERED, ROWS), BF),
            pltpu.VMEM((ROWS, 128), F32),
            pltpu.VMEM((4, ROWS, D), BF),
            pltpu.VMEM((4, ROWS, D), BF),
            pltpu.VMEM((ROWS, FF), F32),
            pltpu.VMEM((ROWS, FF), F32),
            pltpu.VMEM((ROWS, FF), BF),
            pltpu.VMEM((ROWS, 2 * FF), BF),
            pltpu.VMEM((2, GATHERED, D), F32),
            pltpu.VMEM((2, 2, 2, 5, TOK, HALF), BF),
            pltpu.VMEM((NY, 2 * WROWS, FF), F32),
            pltpu.VMEM((2, 2, 5, WROWS, FF), BF),
            dma((NZ,)), dma((NZ,)),
            dma((2, 2, NZ)), dma((2, 2, NZ)),
            dma((4, PEERS)), dma((4, PEERS)),
            dma((2, 2, 2, 5)), dma((2, 2, 2, 5)),
            dma((2, 2, 5)), dma((2, 2, 5)),
        ],
        compiler_params=pltpu.CompilerParams(
            collective_id=0, has_side_effects=True, vmem_limit_bytes=58 * 1024 * 1024
        ),
        cost_estimate=pl.CostEstimate(flops=7_000_000_000, bytes_accessed=8_000_000, transcendentals=400_000),
    )(expert_ids, gate_values, tokens, cotangent, w_gate[0], w_up[0], w_down[0])
    return out, dtok, dg[None], du[None], dd[None]


def solution(mesh):
    rows = P(("dp", "expert"), None)
    weights = P("expert", None, None)
    return jax.shard_map(
        on_device,
        mesh=mesh,
        in_specs=(rows,) * 4 + (weights,) * 3,
        out_specs=(rows, rows, P("expert", "dp", None), P("expert", "dp", None), P("expert", None, "dp")),
        check_vma=False,
    )
```

time: 286 us -> 120 us (0.42)
  waiting for transfers between devices: 169 us -> 0 us
  Pallas kernels: 0 us -> 111 us
  starting transfers between devices: 33.1 us -> 0 us
  local copies, waits for them, and re-layouts: 36.5 us -> 7.15 us
  matrix products: 22.8 us -> 0 us
  between operations: 14.3 us -> 0.67 us
  other arithmetic: 9.23 us -> 0 us
    all_to_all x4 -> x0, waiting for transfers between devices: 169 us -> none  [the longest x1 43.7 us: on_device(): lax.all_to_all(outgoing, 'expert', split_axis=0, concat_axis=0, tiled=True)]
    pallas_call x0 -> x1, Pallas kernels: none -> 111 us  [on_device(): pl.pallas_call(kernel, out_shape=(jax.ShapeDtypeStruct((TOK, D), BF), jax...]
    all_to_all x4 -> x0, starting transfers between devices: 32.8 us -> none  [the longest x1 15 us: on_device(): lax.all_to_all(outgoing, 'expert', split_axis=0, concat_axis=0, tiled=True)]
    dot_general x9 -> x0, matrix products: 22.8 us -> none  [the longest x2 6.87 us: contract(): lax.dot_general(left_side, right_side, (((0,), (0,)), ((), ())), preferre...]
    reshape x8 -> x0, local copies, waits for them, and re-layouts: 19.3 us -> none  [the longest x1 3.61 us: on_device(): input_grads.reshape(experts, capacity, features)]
    scatter x1 -> x0, local copies, waits for them, and re-layouts: 7.59 us -> none  [on_device(): jnp.zeros((experts * capacity, features), jnp.bfloat16).at[target]]
    gather x2 -> x0, local copies, waits for them, and re-layouts: 4.12 us -> none  [the longest x1 2.06 us: on_device(): returned_grads.reshape(experts * capacity, features)[target]]
    unnamed x20 -> x19, local copies, waits for them, and re-layouts: 3.22 us -> 7.15 us
  transfers between devices with their start and end apart: 6 -> 0, of which waited for: 4 -> 0; matrix products, arithmetic and copies ran while one was open for 15% -> 0% of each run, Pallas kernels for 0% -> 0%
where the time goes in v1:
time: 120 us; the launch traced here: 119 us
  Pallas kernels  111 us (92%)
  local copies, waits for them, and re-layouts  7.15 us (6%)
    pallas_call x1, Pallas kernels, on_device(): pl.pallas_call(kernel, out_shape=(jax.ShapeDtypeStruct((TOK, D), BF), jax...  111 us
    unnamed x19, local copies, waits for them, and re-layouts  7.15 us

profile of v1, /device:TPU:1, one launch (start us, length us, event | category | flops | bytes accessed | tf_op | source)
XLA Modules:
  0.0 118.8 jit_solution(13980441940634096556)
XLA Ops:
  0.6 0.0 copy-start.4
  0.6 0.7 copy-done.4
  1.3 0.0 copy-start.5
  1.3 0.7 copy.12.ids_ref
  2.0 0.0 copy-done.5
  2.0 0.7 copy.13.gv_ref
  2.7 111.0 %shard_map.110 = (bf16[64,1024]{1,0:T(8,128)(2,1)}, bf16[64,1024]{1,0:T(8,128)(2,1)}, f32[128,512]{1,0:T(8,128)}, f32[128,512]{1,0:T(8,128)}, f32[512,128]{1,0:T(8,128)}) custom-call(s32[64,8]{1,0:T(8,128)} %copy.12.ids_ref, f32[64,8]{1,0:T(8,128)} %copy.13.gv_ref, bf16[64,1024]{1,0:T(8,128)(2,1)} %tok_ref.1, bf16[64,1024]{1,0:T(8,128)(2,1)} %cot_ref.1, ...), custom_call_target="tpu_custom_call" | custom-call | flops 7000000000 | bytes 8000000 | tf_op jit(solution)/shard_map/pallas_call | solution.py:308
  113.7 0.0 copy-start.3
  113.7 0.0 copy-start.2
  113.7 1.6 %copy.19 = bf16[64,1024]{1,0:T(8,128)(2,1)} copy(bf16[64,1024]{1,0:T(8,128)(2,1)} %get-tuple-element.20) | data formatting | bytes 262144
  115.3 0.0 copy-done.3
  115.3 0.7 copy.20
  116.0 0.0 copy-done.2
  116.0 0.0 copy-start.1
  116.0 0.7 copy.21
  116.7 0.3 copy-done.1
  117.0 0.0 copy-start
  117.0 0.7 copy.22
  117.8 0.3 copy-done
  118.1 0.7 copy.23
Async XLA Ops:
  0.6 0.7 copy-start.4
  1.3 0.7 copy-start.5
  113.7 1.6 %copy-start.3 = (bf16[64,1024]{1,0:T(8,128)(2,1)S(1)}, bf16[64,1024]{1,0:T(8,128)(2,1)}, u32[]{:S(2)}) copy-start(bf16[64,1024]{1,0:T(8,128)(2,1)} %get-tuple-element.21) | copy-start | bytes 393220
  113.7 2.3 %copy-start.2 = (f32[128,512]{1,0:T(8,128)S(1)}, f32[128,512]{1,0:T(8,128)}, u32[]{:S(2)}) copy-start(f32[128,512]{1,0:T(8,128)} %get-tuple-element.12) | copy-start | bytes 786436
  116.0 1.0 copy-start.1
  117.0 1.0 copy-start

commit v2 on v1

v2 whole, which is shorter than its diff:
```python
import jax
import jax.numpy as jnp
from jax import lax
from jax.experimental import pallas as pl
from jax.experimental.pallas import tpu as pltpu
from jax.sharding import PartitionSpec as P

MESH = pl.DeviceIdType.MESH
BF = jnp.bfloat16
F32 = jnp.float32
NX, NZ, NC = 4, 8, 2
NY = 8
TOK = 64
D = 1024
HALF = D // 2
FF = 512
CAP = 10
SLOTS = NZ * CAP
PEERS = NX * NC
ROWS = PEERS * SLOTS
GATHERED = NZ * TOK
EXPERTS = NX * NZ * NC
WIDE = 256
STEPS = ((4, 3), (3, 4))
WSTEPS = ((3, 4), (4, 3), (4, 3))


def nn(a, b):
    return jnp.dot(a, b, preferred_element_type=F32)


def nt(a, b):
    return lax.dot_general(a, b, (((1,), (1,)), ((), ())), preferred_element_type=F32)


def tn(a, b):
    return lax.dot_general(a, b, (((0,), (0,)), ((), ())), preferred_element_type=F32)


def kernel(
    ids_ref, gv_ref, tok_ref, cot_ref, wg_hbm, wu_hbm, wd_hbm,
    out_ref, dtok_ref, dg_ref, du_ref, dd_ref,
    meta, gath, pick, pick_t, pickg_t, gslot, send_x, recv_x, keep_s, keep_d, act, dpre, part, zbuf, wboth, wdown, yboth, ydown, act_t, tok_t, wg_ref, wu_ref, wd_ref,
    m_ss, m_rs, g_ss, g_rs, x_ss, x_rs, z_ss, z_rs, y_ss, y_rs, w_s,
):
    y = lax.axis_index("dp")
    e = lax.axis_index("expert")
    c = e % 2
    z = (e // 2) % NZ
    x = e // (2 * NZ)
    up = (y, (x * NZ + (z + 1) % NZ) * 2 + c)
    down = (y, (x * NZ + (z + NZ - 1) % NZ) * 2 + c)
    y_up = ((y + 1) % NY, e)
    y_down = ((y + NY - 1) % NY, e)

    def peer(j, sign):
        dx, dc = j // 2, j % 2
        return (y, (((x + sign * dx + NX) % NX) * NZ + z) * 2 + (c + dc) % 2)

    loads = [
        pltpu.make_async_copy(src, dst, w_s.at[n])
        for n, (src, dst) in enumerate(((wg_hbm, wg_ref), (wu_hbm, wu_ref), (wd_hbm, wd_ref)))
    ]
    for load in loads:
        load.start()
    barrier = pltpu.get_barrier_semaphore()
    friends = [up, down, y_up, y_down] + [peer(j, 1) for j in range(1, PEERS)]
    for friend in friends:
        pl.semaphore_signal(barrier, inc=1, device_id=friend, device_id_type=MESH)

    line = lax.broadcasted_iota(jnp.int32, (2 * EXPERTS, TOK), 0)
    gate = jnp.zeros((2 * EXPERTS, TOK), F32)
    for k in range(8):
        gate = jnp.where(line % EXPERTS == ids_ref[k : k + 1, :], gv_ref[k : k + 1, :], gate)
    gate = gate.T
    lane = lax.broadcasted_iota(jnp.int32, (TOK, 2 * EXPERTS), 1)
    high = gate.astype(BF).astype(F32)
    meta[0] = jnp.where(lane < EXPERTS, high, gate - high).astype(BF)
    for h in range(2):
        gath[0, h, 0] = tok_ref[:, h * HALF : (h + 1) * HALF]
        gath[1, h, 0] = cot_ref[:, h * HALF : (h + 1) * HALF]

    pl.semaphore_wait(barrier, len(friends))

    started = []

    def send(src, dst, ss, rs, to):
        copy = pltpu.make_async_remote_copy(
            src_ref=src, dst_ref=dst, send_sem=ss, recv_sem=rs, device_id=to, device_id_type=MESH
        )
        copy.start()
        started.append(copy)
        return copy

    def gather_step(buf, ss, rs, steps, s, prev):
        now = []
        for way, (to, count) in enumerate(zip((up, down), steps)):
            if s > count:
                now.append(None)
                continue
            if s > 1:
                prev[way].wait_recv()
            src = (NZ - s + 1) % NZ if way == 0 else s - 1
            dst = NZ - s if way == 0 else s
            now.append(send(buf.at[src], buf.at[dst], ss.at[dst], rs.at[dst], to))
        return [n if n is not None else p for n, p in zip(now, prev or (None, None))]

    m_last, t_last, c_last = None, [None, None], [None, None]
    for s in range(1, 5):
        m_last = gather_step(meta, m_ss, m_rs, STEPS[0], s, m_last)
        for h in range(2):
            t_last[h] = gather_step(gath.at[0, h], g_ss.at[0, h], g_rs.at[0, h], STEPS[h], s, t_last[h])
    for h in range(2):
        c_last[h] = gather_step(gath.at[1, h], g_ss.at[1, h], g_rs.at[1, h], STEPS[h], 1, None)

    for way in range(2):
        m_last[way].wait_recv()
    row = lax.broadcasted_iota(jnp.int32, (16, 2 * EXPERTS), 0)
    col = lax.broadcasted_iota(jnp.int32, (16, 2 * EXPERTS), 1)
    wanted = (((x + (row % PEERS) // 2) % NX) * NZ + z) * 2 + (c + row) % 2
    chosen = jnp.where(col % EXPERTS == wanted, 1.0, 0.0).astype(BF)
    gate_row = nt(chosen, meta[...].reshape(GATHERED, 2 * EXPERTS))
    match = jnp.where(gate_row > 0.0, 1.0, 0.0)
    first = lax.broadcasted_iota(jnp.int32, (GATHERED, GATHERED), 0)
    second = lax.broadcasted_iota(jnp.int32, (GATHERED, GATHERED), 1)
    rank = nn(match.astype(BF), jnp.where(first < second, 1.0, 0.0).astype(BF))
    place = jnp.where(gate_row > 0.0, rank, -1.0)
    slot = lax.broadcasted_iota(jnp.int32, (SLOTS, GATHERED), 0).astype(F32)
    for j in range(PEERS):
        hit = slot == place[j : j + 1, :]
        pick[j * SLOTS : (j + 1) * SLOTS, :] = jnp.where(hit, 1.0, 0.0).astype(BF)
        weight = jnp.sum(jnp.where(hit, gate_row[j : j + 1, :], 0.0), axis=1, keepdims=True)
        gslot[j * SLOTS : (j + 1) * SLOTS, :] = jnp.broadcast_to(weight, (SLOTS, 128))

    for h in range(2):
        for way in range(2):
            t_last[h][way].wait_recv()

    def chunks(count, body):
        def step(i, carry):
            body(pl.ds(pl.multiple_of(i * WIDE, WIDE), WIDE))
            return carry

        lax.fori_loop(0, count, step, 0)

    def exchange(n, sign, begin=0, width=D):
        sem = 4 if begin else n
        cols = pl.ds(begin, width)
        recv_x[n, 0:SLOTS, cols] = send_x[n, 0:SLOTS, cols]
        copies = []
        for j in (4, 5, 2, 3, 6, 7, 1):
            block = pl.ds(j * SLOTS, SLOTS)
            src, dst = send_x.at[n, block, cols], recv_x.at[n, block, cols]
            copies.append(send(src, dst, x_ss.at[sem, j], x_rs.at[sem, j], peer(j, sign)))
        return copies

    def picked(a, h):
        source = gath[a, h].reshape(GATHERED, HALF)
        return nn(pick[...], source)

    for h in range(2):
        send_x[0, :, h * HALF : (h + 1) * HALF] = picked(0, h).astype(BF)
    tok_moves = exchange(0, 1)

    for s in range(2, 5):
        for h in range(2):
            c_last[h] = gather_step(gath.at[1, h], g_ss.at[1, h], g_rs.at[1, h], STEPS[h], s, c_last[h])
    for h in range(2):
        for way in range(2):
            c_last[h][way].wait_recv()

    for h in range(2):
        send_x[1, :, h * HALF : (h + 1) * HALF] = (picked(1, h) * gslot[:, 0:1]).astype(BF)
    cot_moves = exchange(1, 1)

    for q in range(4):
        cols = slice(q * 128, (q + 1) * 128)
        plain = pick[:, cols].astype(F32)
        pick_t[cols, :] = plain.T.astype(BF)
        pickg_t[cols, :] = (plain * gslot[...]).T.astype(BF)

    for load in loads:
        load.wait()
    for move in tok_moves:
        move.wait_recv()

    def forward(cols):
        g = nn(recv_x[0], wg_ref[:, cols])
        u = nn(recv_x[0], wu_ref[:, cols])
        s = jax.nn.sigmoid(g)
        silu = g * s
        keep_s[:, cols] = silu
        keep_d[:, cols] = u * s * (1.0 + g * (1.0 - s))
        act[:, cols] = (silu * u).astype(BF)

    def forward_out(cols):
        send_x[2, :, cols] = nn(act[...], wd_ref[:, cols]).astype(BF)

    chunks(FF // WIDE, forward)
    chunks(D // WIDE, forward_out)
    out_moves = exchange(2, -1)
    for q in range(FF // 128):
        act_t[q * 128 : (q + 1) * 128, :] = act[:, q * 128 : (q + 1) * 128].astype(F32).T.astype(BF)
    for q in range(D // 128):
        tok_t[q * 128 : (q + 1) * 128, :] = recv_x[0, :, q * 128 : (q + 1) * 128].astype(F32).T.astype(BF)
    for move in cot_moves:
        move.wait_recv()

    def weight_down(cols):
        wdown[:, cols] = nn(act_t[...], recv_x[1, :, cols])

    def weight_both(cols):
        wboth[:, cols] = nn(tok_t[...], dpre[:, cols])

    def reduce_step(buf, ss, rs, ways, steps, h, s, prev, own):
        now = []
        for way in range(2):
            count = steps[way]
            if s > count:
                now.append(prev[way])
                continue
            ahead = count + 1 - s
            term = own(ahead if way == 0 else 8 - ahead, h)
            if s > 1:
                prev[way].wait_recv()
                term = term + buf(h, way, s - 1)[...].astype(F32)
            buf(h, way, s - 1)[...] = term.astype(BF)
            now.append(
                send(buf(h, way, s - 1), buf(h, way, s), ss.at[h, way, s], rs.at[h, way, s], ways[way])
            )
        return now

    def reduce_end(buf, steps, h, prev, own):
        for way in range(2):
            prev[way].wait_recv()
        first, second = steps
        return own(0, h) + buf(h, 0, first)[...].astype(F32) + buf(h, 1, second)[...].astype(F32)

    def own_w(k, n):
        there = pl.ds(pl.multiple_of(((y + k) % NY) * 128, 128), 128)
        if n == 2:
            return wdown[:, there]
        return wboth[there, n * FF : (n + 1) * FF]

    def own_part(a):
        return lambda k, h: part[a, k * TOK : (k + 1) * TOK, h * HALF : (h + 1) * HALF]

    def y_buf(n, way, s):
        return ydown.at[way, s] if n == 2 else yboth.at[n, way, s]

    def z_buf(a):
        return lambda h, way, s: zbuf.at[a, h, way, s]

    y_last, z_last = [None] * 3, [[None, None], [None, None]]

    def y_step(n, s):
        y_last[n] = reduce_step(y_buf, y_ss, y_rs, (y_up, y_down), WSTEPS[n], n, s, y_last[n], own_w)

    def y_end(n):
        return reduce_end(y_buf, WSTEPS[n], n, y_last[n], own_w)

    def z_step(a, s, halves=(0, 1)):
        for h in halves:
            z_last[a][h] = reduce_step(
                z_buf(a), z_ss.at[a], z_rs.at[a], (up, down), STEPS[h], h, s, z_last[a][h], own_part(a)
            )

    def combine(a, weights, moves, begin=0, width=D):
        for move in moves:
            move.wait_recv()

        def summed(cols):
            part[a, :, cols] = nn(weights[...], recv_x[2 + a, :, cols])

        def step(i, carry):
            summed(pl.ds(pl.multiple_of(begin + i * WIDE, WIDE), WIDE))
            return carry

        lax.fori_loop(0, width // WIDE, step, 0)

    def z_end(a, h, result):
        total = reduce_end(z_buf(a), STEPS[h], h, z_last[a][h], own_part(a))
        result[:, h * HALF : (h + 1) * HALF] = total.astype(BF)

    def backward(cols):
        da = nt(recv_x[1], wd_ref[cols, :])
        dpre[:, cols] = (da * keep_d[:, cols]).astype(BF)
        dpre[:, pl.ds(pl.multiple_of(cols.start + FF, WIDE), WIDE)] = (da * keep_s[:, cols]).astype(BF)

    def backward_in(cols):
        both = nt(dpre[:, 0:FF], wg_ref[cols, :]) + nt(dpre[:, FF : 2 * FF], wu_ref[cols, :])
        send_x[3, :, cols] = both.astype(BF)

    chunks(D // WIDE, weight_down)
    y_step(2, 1)
    chunks(FF // WIDE, backward)
    chunks(D // WIDE, backward_in)
    grad_moves = [exchange(3, -1, h * HALF, HALF) for h in range(2)]
    chunks(2 * FF // WIDE, weight_both)
    y_step(0, 1)
    y_step(1, 1)
    y_step(2, 2)
    combine(0, pickg_t, out_moves)
    z_step(0, 1)
    y_step(0, 2)
    y_step(1, 2)
    z_step(0, 2)
    y_step(2, 3)
    z_step(0, 3)
    combine(1, pick_t, grad_moves[0], 0, HALF)
    z_step(1, 1, (0,))
    y_step(0, 3)
    z_step(0, 4)
    y_step(1, 3)
    z_step(1, 2, (0,))
    for h in range(2):
        z_end(0, h, out_ref)
    y_step(2, 4)
    z_step(1, 3, (0,))
    combine(1, pick_t, grad_moves[1], HALF, HALF)
    z_step(1, 1, (1,))
    z_step(1, 4, (0,))
    y_step(0, 4)
    z_step(1, 2, (1,))
    y_step(1, 4)
    z_step(1, 3, (1,))
    z_end(1, 0, dtok_ref)
    dd_ref[...] = y_end(2)
    z_step(1, 4, (1,))
    dg_ref[...] = y_end(0)
    du_ref[...] = y_end(1)
    z_end(1, 1, dtok_ref)

    for copy in started:
        copy.wait_send()


def place(*refs):
    for src, dst in zip(refs[:5], refs[5:]):
        dst[...] = src[...]


def on_device(tokens, expert_ids, gate_values, cotangent, w_gate, w_up, w_down):
    vmem = pl.BlockSpec(memory_space=pltpu.VMEM)
    hbm = pl.BlockSpec(memory_space=pl.ANY)
    dma = pltpu.SemaphoreType.DMA
    shapes = (
        jax.ShapeDtypeStruct((TOK, D), BF),
        jax.ShapeDtypeStruct((TOK, D), BF),
        jax.ShapeDtypeStruct((128, FF), F32),
        jax.ShapeDtypeStruct((128, FF), F32),
        jax.ShapeDtypeStruct((FF, 128), F32),
    )
    results = pl.pallas_call(
        kernel,
        out_shape=shapes,
        in_specs=[vmem] * 4 + [hbm] * 3,
        out_specs=(vmem,) * 5,
        scratch_shapes=[
            pltpu.VMEM((NZ, TOK, 2 * EXPERTS), BF),
            pltpu.VMEM((2, 2, NZ, TOK, HALF), BF),
            pltpu.VMEM((ROWS, GATHERED), BF),
            pltpu.VMEM((GATHERED, ROWS), BF),
            pltpu.VMEM((GATHERED, ROWS), BF),
            pltpu.VMEM((ROWS, 128), F32),
            pltpu.VMEM((4, ROWS, D), BF),
            pltpu.VMEM((4, ROWS, D), BF),
            pltpu.VMEM((ROWS, FF), F32),
            pltpu.VMEM((ROWS, FF), F32),
            pltpu.VMEM((ROWS, FF), BF),
            pltpu.VMEM((ROWS, 2 * FF), BF),
            pltpu.VMEM((2, GATHERED, D), F32),
            pltpu.VMEM((2, 2, 2, 5, TOK, HALF), BF),
            pltpu.VMEM((D, 2 * FF), F32),
            pltpu.VMEM((FF, D), F32),
            pltpu.VMEM((2, 2, 5, 128, FF), BF),
            pltpu.VMEM((2, 5, FF, 128), BF),
            pltpu.VMEM((FF, ROWS), BF),
            pltpu.VMEM((D, ROWS), BF),
            pltpu.VMEM((D, FF), BF),
            pltpu.VMEM((D, FF), BF),
            pltpu.VMEM((FF, D), BF),
            dma((NZ,)), dma((NZ,)),
            dma((2, 2, NZ)), dma((2, 2, NZ)),
            dma((5, PEERS)), dma((5, PEERS)),
            dma((2, 2, 2, 5)), dma((2, 2, 2, 5)),
            dma((3, 2, 5)), dma((3, 2, 5)),
            dma((3,)),
        ],
        compiler_params=pltpu.CompilerParams(
            collective_id=0, has_side_effects=True, vmem_limit_bytes=58 * 1024 * 1024
        ),
        cost_estimate=pl.CostEstimate(flops=7_000_000_000, bytes_accessed=8_000_000, transcendentals=400_000),
    )(expert_ids.T, gate_values.T, tokens, cotangent, w_gate[0], w_up[0], w_down[0])
    out, dtok, dg, du, dd = pl.pallas_call(
        place,
        out_shape=shapes,
        in_specs=[vmem] * 5,
        out_specs=(vmem,) * 5,
    )(*results)
    return out, dtok, dg[None], du[None], dd[None]


def solution(mesh):
    rows = P(("dp", "expert"), None)
    weights = P("expert", None, None)
    return jax.shard_map(
        on_device,
        mesh=mesh,
        in_specs=(rows,) * 4 + (weights,) * 3,
        out_specs=(rows, rows, P("expert", "dp", None), P("expert", "dp", None), P("expert", None, "dp")),
        check_vma=False,
    )
```

time: 120 us -> 115 us (0.958)
  local copies, waits for them, and re-layouts: 7.15 us -> 0 us
  Pallas kernels: 111 us -> 114 us
    unnamed x19 -> x0, local copies, waits for them, and re-layouts: 7.15 us -> none
    pallas_call x1 -> x2, Pallas kernels: 111 us -> 114 us  [the longest x1 112 us: on_device(): pl.pallas_call(kernel, out_shape=shapes, in_specs=[vmem] * 4 + [hbm] * 3,...]
where the time goes in v2:
time: 115 us; the launch traced here: 114 us
  Pallas kernels  114 us (99%)
    pallas_call x1, Pallas kernels, on_device(): pl.pallas_call(kernel, out_shape=shapes, in_specs=[vmem] * 4 + [hbm] * 3,...  112 us

profile of v2, /device:TPU:1, one launch (start us, length us, event | category | flops | bytes accessed | tf_op | source)
XLA Modules:
  0.0 114.4 jit_solution(14384053079942949378)
XLA Ops:
  0.6 111.6 %shard_map.110 = (bf16[64,1024]{1,0:T(8,128)(2,1)}, bf16[64,1024]{1,0:T(8,128)(2,1)}, f32[128,512]{1,0:T(8,128)}, f32[128,512]{1,0:T(8,128)}, f32[512,128]{1,0:T(8,128)}) custom-call(s32[8,64]{1,0:T(8,128)} %bitcast.14, f32[8,64]{1,0:T(8,128)} %bitcast.15, bf16[64,1024]{1,0:T(8,128)(2,1)} %tok_ref.1, bf16[64,1024]{1,0:T(8,128)(2,1)} %cot_ref.1, ...), custom_call_target="tpu_custom_call" | custom-call | flops 7000000000 | bytes 8000000 | tf_op jit(solution)/shard_map/pallas_call | solution.py:354
  112.2 2.2 %shard_map.111 = (bf16[64,1024]{1,0:T(8,128)(2,1)}, bf16[64,1024]{1,0:T(8,128)(2,1)}, f32[128,512]{1,0:T(8,128)}, f32[128,512]{1,0:T(8,128)}, f32[512,128]{1,0:T(8,128)}) custom-call(bf16[64,1024]{1,0:T(8,128)(2,1)} %get-tuple-element.15.refs_0_, bf16[64,1024]{1,0:T(8,128)(2,1)} %get-tuple-element.16.refs_1_, f32[128,512]{1,0:T(8,128)} %get-tuple-element.17.refs_2_, ...), custom_call_target="tpu_custom_call" | custom-call | tf_op jit(solution)/shard_map/pallas_call | solution.py:395

commit v3 on v2

--- a/solution.py
+++ b/solution.py
@@ -305,31 +305,31 @@
     y_step(0, 2)
     y_step(1, 2)
     z_step(0, 2)
+    combine(1, pick_t, grad_moves[0], 0 * HALF, HALF)
+    z_step(1, 1, (0,))
     y_step(2, 3)
     z_step(0, 3)
-    combine(1, pick_t, grad_moves[0], 0, HALF)
-    z_step(1, 1, (0,))
+    z_step(1, 2, (0,))
+    combine(1, pick_t, grad_moves[1], 1 * HALF, HALF)
+    z_step(1, 1, (1,))
+    z_step(0, 4)
+    z_step(1, 3, (0,))
     y_step(0, 3)
-    z_step(0, 4)
+    z_step(1, 2, (1,))
     y_step(1, 3)
-    z_step(1, 2, (0,))
     for h in range(2):
         z_end(0, h, out_ref)
+    z_step(1, 4, (0,))
     y_step(2, 4)
-    z_step(1, 3, (0,))
-    combine(1, pick_t, grad_moves[1], HALF, HALF)
-    z_step(1, 1, (1,))
-    z_step(1, 4, (0,))
+    z_step(1, 3, (1,))
     y_step(0, 4)
-    z_step(1, 2, (1,))
+    z_step(1, 4, (1,))
     y_step(1, 4)
-    z_step(1, 3, (1,))
     z_end(1, 0, dtok_ref)
     dd_ref[...] = y_end(2)
-    z_step(1, 4, (1,))
     dg_ref[...] = y_end(0)
+    z_end(1, 1, dtok_ref)
     du_ref[...] = y_end(1)
-    z_end(1, 1, dtok_ref)
 
     for copy in started:
         copy.wait_send()

time: 115 us -> 112 us (0.974)
  Pallas kernels: 114 us -> 111 us
    pallas_call x1, Pallas kernels: 112 us -> 109 us  [on_device(): pl.pallas_call(kernel, out_shape=shapes, in_specs=[vmem] * 4 + [hbm] * 3,...]
where the time goes in v3:
time: 112 us
  Pallas kernels  111 us (99%)
    pallas_call x1, Pallas kernels, on_device(): pl.pallas_call(kernel, out_shape=shapes, in_specs=[vmem] * 4 + [hbm] * 3,...  109 us

profile of v3, /device:TPU:1, one launch (start us, length us, event | category | flops | bytes accessed | tf_op | source)
XLA Modules:
  0.0 112.0 jit_solution(997263196574818924)
XLA Ops:
  0.6 109.1 %shard_map.110 = (bf16[64,1024]{1,0:T(8,128)(2,1)}, bf16[64,1024]{1,0:T(8,128)(2,1)}, f32[128,512]{1,0:T(8,128)}, f32[128,512]{1,0:T(8,128)}, f32[512,128]{1,0:T(8,128)}) custom-call(s32[8,64]{1,0:T(8,128)} %bitcast.14, f32[8,64]{1,0:T(8,128)} %bitcast.15, bf16[64,1024]{1,0:T(8,128)(2,1)} %tok_ref.1, bf16[64,1024]{1,0:T(8,128)(2,1)} %cot_ref.1, ...), custom_call_target="tpu_custom_call" | custom-call | flops 7000000000 | bytes 8000000 | tf_op jit(solution)/shard_map/pallas_call | solution.py:354
  109.8 2.2 %shard_map.111 = (bf16[64,1024]{1,0:T(8,128)(2,1)}, bf16[64,1024]{1,0:T(8,128)(2,1)}, f32[128,512]{1,0:T(8,128)}, f32[128,512]{1,0:T(8,128)}, f32[512,128]{1,0:T(8,128)}) custom-call(bf16[64,1024]{1,0:T(8,128)(2,1)} %get-tuple-element.15.refs_0_, bf16[64,1024]{1,0:T(8,128)(2,1)} %get-tuple-element.16.refs_1_, f32[128,512]{1,0:T(8,128)} %get-tuple-element.17.refs_2_, ...), custom_call_target="tpu_custom_call" | custom-call | tf_op jit(solution)/shard_map/pallas_call | solution.py:395

commit v4 on v3

--- a/solution.py
+++ b/solution.py
@@ -129,12 +129,6 @@
     for j in range(PEERS):
         hit = slot == place[j : j + 1, :]
         pick[j * SLOTS : (j + 1) * SLOTS, :] = jnp.where(hit, 1.0, 0.0).astype(BF)
-        weight = jnp.sum(jnp.where(hit, gate_row[j : j + 1, :], 0.0), axis=1, keepdims=True)
-        gslot[j * SLOTS : (j + 1) * SLOTS, :] = jnp.broadcast_to(weight, (SLOTS, 128))
-
-    for h in range(2):
-        for way in range(2):
-            t_last[h][way].wait_recv()
 
     def chunks(count, body):
         def step(i, carry):
@@ -144,7 +138,7 @@
         lax.fori_loop(0, count, step, 0)
 
     def exchange(n, sign, begin=0, width=D):
-        sem = 4 if begin else n
+        sem = 2 * n + (begin > 0)
         cols = pl.ds(begin, width)
         recv_x[n, 0:SLOTS, cols] = send_x[n, 0:SLOTS, cols]
         copies = []
@@ -158,20 +152,26 @@
         source = gath[a, h].reshape(GATHERED, HALF)
         return nn(pick[...], source)
 
+    tok_moves = []
     for h in range(2):
+        for way in range(2):
+            t_last[h][way].wait_recv()
         send_x[0, :, h * HALF : (h + 1) * HALF] = picked(0, h).astype(BF)
-    tok_moves = exchange(0, 1)
+        tok_moves += exchange(0, 1, h * HALF, HALF)
+    for j in range(PEERS):
+        hit = slot == place[j : j + 1, :]
+        weight = jnp.sum(jnp.where(hit, gate_row[j : j + 1, :], 0.0), axis=1, keepdims=True)
+        gslot[j * SLOTS : (j + 1) * SLOTS, :] = jnp.broadcast_to(weight, (SLOTS, 128))
 
     for s in range(2, 5):
         for h in range(2):
             c_last[h] = gather_step(gath.at[1, h], g_ss.at[1, h], g_rs.at[1, h], STEPS[h], s, c_last[h])
+    cot_moves = []
     for h in range(2):
         for way in range(2):
             c_last[h][way].wait_recv()
-
-    for h in range(2):
         send_x[1, :, h * HALF : (h + 1) * HALF] = (picked(1, h) * gslot[:, 0:1]).astype(BF)
-    cot_moves = exchange(1, 1)
+        cot_moves += exchange(1, 1, h * HALF, HALF)
 
     for q in range(4):
         cols = slice(q * 128, (q + 1) * 128)
@@ -382,7 +382,7 @@
             pltpu.VMEM((FF, D), BF),
             dma((NZ,)), dma((NZ,)),
             dma((2, 2, NZ)), dma((2, 2, NZ)),
-            dma((5, PEERS)), dma((5, PEERS)),
+            dma((8, PEERS)), dma((8, PEERS)),
             dma((2, 2, 2, 5)), dma((2, 2, 2, 5)),
             dma((3, 2, 5)), dma((3, 2, 5)),
             dma((3,)),

time: 112 us -> 110 us (0.982); the launches traced: 112 us -> 109 us
  Pallas kernels: 111 us -> 108 us
    pallas_call x1, Pallas kernels: 109 us -> 106 us  [on_device(): pl.pallas_call(kernel, out_shape=shapes, in_specs=[vmem] * 4 + [hbm] * 3,...]
where the time goes in v4:
time: 110 us; the launch traced here: 109 us
  Pallas kernels  108 us (98%)
    pallas_call x1, Pallas kernels, on_device(): pl.pallas_call(kernel, out_shape=shapes, in_specs=[vmem] * 4 + [hbm] * 3,...  106 us
    pallas_call x1, Pallas kernels, on_device(): pl.pallas_call(place, out_shape=shapes, in_specs=[vmem] * 5, out_specs=(v...  2.22 us

profile of v4, /device:TPU:1, one launch (start us, length us, event | category | flops | bytes accessed | tf_op | source)
XLA Modules:
  0.0 108.6 jit_solution(7009620572551658787)
XLA Ops:
  0.6 105.8 %shard_map.110 = (bf16[64,1024]{1,0:T(8,128)(2,1)}, bf16[64,1024]{1,0:T(8,128)(2,1)}, f32[128,512]{1,0:T(8,128)}, f32[128,512]{1,0:T(8,128)}, f32[512,128]{1,0:T(8,128)}) custom-call(s32[8,64]{1,0:T(8,128)} %bitcast.14, f32[8,64]{1,0:T(8,128)} %bitcast.15, bf16[64,1024]{1,0:T(8,128)(2,1)} %tok_ref.1, bf16[64,1024]{1,0:T(8,128)(2,1)} %cot_ref.1, ...), custom_call_target="tpu_custom_call" | custom-call | flops 7000000000 | bytes 8000000 | tf_op jit(solution)/shard_map/pallas_call | solution.py:354
  106.4 2.2 %shard_map.111 = (bf16[64,1024]{1,0:T(8,128)(2,1)}, bf16[64,1024]{1,0:T(8,128)(2,1)}, f32[128,512]{1,0:T(8,128)}, f32[128,512]{1,0:T(8,128)}, f32[512,128]{1,0:T(8,128)}) custom-call(bf16[64,1024]{1,0:T(8,128)(2,1)} %get-tuple-element.15.refs_0_, bf16[64,1024]{1,0:T(8,128)(2,1)} %get-tuple-element.16.refs_1_, f32[128,512]{1,0:T(8,128)} %get-tuple-element.17.refs_2_, ...), custom_call_target="tpu_custom_call" | custom-call | tf_op jit(solution)/shard_map/pallas_call | solution.py:395
